TPU v7x, 1024 devices: a whole 4x8x16 slice. The times are simulated.
1024 devices in a mesh: band: 16 (over z_hi, x), tr: 8 (over z_lo, core), tc: 8 (over y).
Axes of the slice: x: 4, y: 8, z: 16 (z_hi: 4, z_lo: 4; z = z_hi * 4 + z_lo), core: 2. Of those that a mesh axis runs over, the one named last changes fastest.
Arguments:
- voltages: bfloat16 [131072, 2, 1024], P(('band', 'tr', 'tc')), parts along dimension 0, may hold values from -4 to 4
Outputs:
- visibilities: bfloat16 [512, 2, 1024, 1024], P(('band', 'tc'), None, 'tr'), parts along dimension 0
There are 16 independent parts, one for each index of `band`. A program takes and returns all parts, laid end to end along the dimension named above; each array names one. Nothing has to cross between parts.
All inputs are finite; a program needn't handle non-finite values.
Results may differ from a plain program's by a relative error of at most 0.0054.
Values may be sent and summed in bfloat16 or wider, within the bound.
A program may use at most 32 MiB of HBM per device.

v0:
```python
import math

import jax
import jax.numpy as jnp
from jax import lax
from jax.sharding import PartitionSpec as P

FINE = 32
TAPS = 16


def shifted(block, axis, distance):
    devices = range(lax.axis_size(axis))
    route = [(i - distance, i) for i in devices if i - distance in devices]
    return lax.ppermute(block, axis, route)


def filter_taps(tap_total, fine_total):
    length = tap_total * fine_total
    position = jnp.arange(length).astype(jnp.float32)
    offset = (position - (length - 1) / 2.0) / fine_total
    prototype = jnp.sin(math.pi * offset) / (math.pi * offset)
    prototype = prototype / jnp.sqrt(jnp.sum(prototype * prototype))
    return prototype.reshape(tap_total, fine_total)


def fourier_table(fine_total):
    indices = jnp.arange(fine_total).astype(jnp.float32)
    angles = 2.0 * math.pi * jnp.mod(indices[:, None] * indices[None, :], fine_total) / fine_total
    cosine = jnp.cos(angles)
    sine_part = jnp.sin(angles)
    stacked = jnp.stack(
        [jnp.stack([cosine, -sine_part], axis=-1), jnp.stack([sine_part, cosine], axis=-1)], axis=1
    )
    return stacked.reshape(2 * fine_total, 2 * fine_total)


def filterbank(extended, hop_count):
    inputs = extended.shape[3]
    tap_table = filter_taps(TAPS, FINE)
    fourier = fourier_table(FINE)
    weighted = jnp.zeros((hop_count, FINE, 2, inputs), jnp.float32)
    for tap_index in range(TAPS):
        weighted = weighted + tap_table[tap_index][None, :, None, None] * extended[
            tap_index : tap_index + hop_count
        ].astype(jnp.float32)
    spectra = jnp.einsum(
        "sjm,jo->som",
        weighted.reshape(hop_count, 2 * FINE, inputs),
        fourier,
        precision=lax.Precision.HIGHEST,
    )
    return spectra.reshape(hop_count, FINE, 2, inputs).astype(jnp.bfloat16)


def per_device(voltages):
    samples = voltages.shape[0]
    inputs = voltages.shape[2]
    hop_count = samples // FINE
    needed = TAPS - 1
    shift_count = (needed + hop_count - 1) // hop_count
    earlier = []
    for distance in range(1, shift_count + 1):
        take_hops = min(hop_count, needed - (distance - 1) * hop_count)
        portion = voltages[samples - take_hops * FINE :]
        arrived = shifted(portion, ("tr", "tc"), distance)
        earlier = [arrived] + earlier
    extended = jnp.concatenate(earlier + [voltages], axis=0).reshape(
        needed + hop_count, FINE, 2, inputs
    )
    spectra = filterbank(extended, hop_count)
    turned = lax.all_to_all(
        lax.all_to_all(spectra, "tr", split_axis=3, concat_axis=0, tiled=True),
        "tc",
        split_axis=1,
        concat_axis=0,
        tiled=True,
    )
    spectra_total = turned.shape[0]
    swapped = jnp.stack([turned[:, :, 1], -turned[:, :, 0]], axis=2)
    stacked = jnp.stack([turned, swapped], axis=0)
    inverse_total = 1.0 / float(spectra_total)
    product = jnp.einsum(
        "rskci,skcj->krij",
        stacked,
        lax.all_gather(turned, "tr", axis=3, tiled=True),
        preferred_element_type=jnp.float32,
    )
    summed = product * inverse_total
    return summed.astype(jnp.bfloat16)


def solution(mesh):
    in_specs = (P(("band", "tr", "tc"), None, None),)
    out_specs = P(("band", "tc"), None, "tr", None)
    return jax.shard_map(
        per_device, mesh=mesh, in_specs=in_specs, out_specs=out_specs, check_vma=False
    )
```

profile of v0, /device:TPU:1, one launch (start us, length us, event | category | flops | bytes accessed | tf_op | source)
XLA Modules:
  0.0 249.5 jit_solution(5302841673824211565)
XLA Ops:
  6.5 4.0 %collective-permute-start.3 = (bf16[128,2,1024]{2,1,0:T(2,128)(2,1)}, bf16[128,2,1024]{2,1,0:T(2,128)(2,1)S(1)}, u32[]{:S(2)}, u32[]{:S(2)}) collective-permute-start(bf16[128,2,1024]{2,1,0:T(2,128)(2,1)} %param.1), channel_id=1, source_target_pairs={{0,1},{1,2},{2,3},{3,4},{4,5},{5,6},{6,7},{7,8},{8,9},{9,10},{10,1... | collective-permute-start | bytes 1572872 | tf_op jit(solution)/shard_map/ppermute | solution.py:15
  10.6 4.2 %collective-permute-start.2 = (bf16[128,2,1024]{2,1,0:T(2,128)(2,1)}, bf16[128,2,1024]{2,1,0:T(2,128)(2,1)S(1)}, u32[]{:S(2)}, u32[]{:S(2)}) collective-permute-start(bf16[128,2,1024]{2,1,0:T(2,128)(2,1)} %param.1), channel_id=1, source_target_pairs={{0,2},{1,3},{2,4},{3,5},{4,6},{5,7},{6,8},{7,9},{8,10},{9,11},{10,... | collective-permute-start | bytes 1572872 | tf_op jit(solution)/shard_map/ppermute | solution.py:15
  14.8 4.6 %collective-permute-start.1 = (bf16[128,2,1024]{2,1,0:T(2,128)(2,1)}, bf16[128,2,1024]{2,1,0:T(2,128)(2,1)S(1)}, u32[]{:S(2)}, u32[]{:S(2)}) collective-permute-start(bf16[128,2,1024]{2,1,0:T(2,128)(2,1)} %param.1), channel_id=1, source_target_pairs={{0,3},{1,4},{2,5},{3,6},{4,7},{5,8},{6,9},{7,10},{8,11},{9,12},{10... | collective-permute-start | bytes 1572872 | tf_op jit(solution)/shard_map/ppermute | solution.py:15
  19.4 2.0 slice.142
  21.5 6.3 %collective-permute-start = (bf16[96,2,1024]{2,1,0:T(2,128)(2,1)}, bf16[96,2,1024]{2,1,0:T(2,128)(2,1)S(1)}, u32[]{:S(2)}, u32[]{:S(2)}) collective-permute-start(bf16[96,2,1024]{2,1,0:T(2,128)(2,1)} %slice.142), channel_id=1, source_target_pairs={{0,4},{1,5},{2,6},{3,7},{4,8},{5,9},{6,10},{7,11},{8,12},{9,13},{1... | collective-permute-start | bytes 1179656 | tf_op jit(solution)/shard_map/ppermute | solution.py:15
  27.8 0.7 multiply_reduce_fusion
  30.3 0.7 mul.340
  31.0 0.7 mul.336
  32.2 0.6 mul.328
  32.9 0.6 mul.324
  33.5 0.7 mul.320
  34.1 0.6 mul.316
  34.8 0.7 mul.312
  36.0 0.7 mul.304
  36.7 0.7 mul.300
  37.4 0.6 pad_maximum_fusion.1
  38.0 1.3 copy.18
  39.3 1.2 reshape.353
  40.5 44.7 %collective-permute-done = bf16[96,2,1024]{2,1,0:T(2,128)(2,1)S(1)} collective-permute-done((bf16[96,2,1024]{2,1,0:T(2,128)(2,1)}, bf16[96,2,1024]{2,1,0:T(2,128)(2,1)S(1)}, u32[]{:S(2)}, u32[]{:S(2)}) %collective-permute-start) | collective-permute-done | bytes 393248 | tf_op jit(solution)/shard_map/ppermute | solution.py:15
  87.8 8.5 %multiply_add_fusion = f32[128,2,1024]{2,1,0:T(2,128)S(1)} fusion(bf16[128,2,1024]{2,1,0:T(2,128)(2,1)S(1)} %copy-done, bf16[128,2,1024]{2,1,0:T(2,128)(2,1)S(1)} %collective-permute-done.3, bf16[128,2,1024]{2,1,0:T(2,128)(2,1)S(1)} %collective-permute-done.2, bf16[128,2,1024]{2,1,0:T(2,128)(2,1)S(1)} %collective-permute-done.1, f32[128]{0:T(128)S(1)} %mul.356, ...), kind=kLoop, calls=%fused_computation.8 | loop fusion | flops 12320768 | bytes 9445376 | tf_op jit(solution)/shard_map/add | solution.py:44
  96.2 0.7 add.121
  97.0 1.0 fusion.5
  98.2 1.9 copy.20
  100.1 2.0 reshape.354
  102.1 47.8 %all_to_all.36 = bf16[8,2,16384]{2,1,0:T(2,128)(2,1)S(1)} all-to-all(bf16[8,2,16384]{2,1,0:T(2,128)(2,1)S(1)} %reshape.354), channel_id=1, replica_groups=mesh['band'=16,'tr'=8,'tc'=8] {'tr'}, dimensions={0} | all-to-all | bytes 1048576 | tf_op jit(solution)/shard_map/all_to_all | solution.py:73
  149.9 1.0 reshape.355
  151.0 1.5 copy.34
  153.0 18.2 %all_to_all.37 = bf16[32,32,2,128]{3,2,0,1:T(2,128)(2,1)S(1)} all-to-all(bf16[32,32,2,128]{3,2,0,1:T(2,128)(2,1)S(1)} %copy.23), channel_id=1, replica_groups=mesh['band'=16,'tr'=8,'tc'=8] {'tc'}, dimensions={1} | all-to-all | bytes 1048576 | tf_op jit(solution)/shard_map/all_to_all | solution.py:72
  171.4 0.8 copy.25
  172.2 1.1 fusion.16
  173.4 64.3 %all-gather.2.cloned.1.call-done = bf16[256,4,2,1024]{3,0,2,1:T(8,128)(2,1)} async-done(((bf16[256,4,2,128]{3,0,2,1:T(8,128)(2,1)}), bf16[256,4,2,1024]{3,0,2,1:T(8,128)(2,1)}) %all-gather.2.cloned.1.call-update) | async-done | bytes 4194320 | tf_op jit(solution)/shard_map/all_gather | solution.py:86
  237.6 5.0 %fusion.2 = bf16[4,2,128,1024]{3,2,1,0:T(8,128)(2,1)} fusion(bf16[256,4,2,1024]{3,0,2,1:T(8,128)(2,1)} %all-gather.2.cloned.1.call-done, bf16[1,256,4,2,128]{4,1,3,2,0:T(8,128)(2,1)S(1)} %maximum_bitcast_fusion, bf16[1,256,4,2,128]{4,1,3,2,0:T(8,128)(2,1)} %bitcast.40), kind=kOutput, calls=%fused_computation.3 | convolution fusion | flops 1076363264 | bytes 7340032 | tf_op jit(solution)/shard_map/rskci,skcj->krij/dot_general | solution.py:83
  (46 shorter events, 5.8 us)
Async XLA Ops:
  6.5 231.1 %all-gather.2.cloned.1.call-start = ((), (), s32[]{:S(2)}) async-start(), calls=%async_computation.2 | async-start | bytes 4718592 | tf_op jit(solution)/shard_map/all_gather | solution.py:86
  6.5 80.2 %collective-permute-start.3 = (bf16[128,2,1024]{2,1,0:T(2,128)(2,1)}, bf16[128,2,1024]{2,1,0:T(2,128)(2,1)S(1)}, u32[]{:S(2)}, u32[]{:S(2)}) collective-permute-start(bf16[128,2,1024]{2,1,0:T(2,128)(2,1)} %param.1), channel_id=1, source_target_pairs={{0,1},{1,2},{2,3},{3,4},{4,5},{5,6},{6,7},{7,8},{8,9},{9,10},{10,1... | collective-permute-start | bytes 1572872 | tf_op jit(solution)/shard_map/ppermute | solution.py:15
  10.6 75.6 %collective-permute-start.2 = (bf16[128,2,1024]{2,1,0:T(2,128)(2,1)}, bf16[128,2,1024]{2,1,0:T(2,128)(2,1)S(1)}, u32[]{:S(2)}, u32[]{:S(2)}) collective-permute-start(bf16[128,2,1024]{2,1,0:T(2,128)(2,1)} %param.1), channel_id=1, source_target_pairs={{0,2},{1,3},{2,4},{3,5},{4,6},{5,7},{6,8},{7,9},{8,10},{9,11},{10,... | collective-permute-start | bytes 1572872 | tf_op jit(solution)/shard_map/ppermute | solution.py:15
  14.8 70.7 %collective-permute-start.1 = (bf16[128,2,1024]{2,1,0:T(2,128)(2,1)}, bf16[128,2,1024]{2,1,0:T(2,128)(2,1)S(1)}, u32[]{:S(2)}, u32[]{:S(2)}) collective-permute-start(bf16[128,2,1024]{2,1,0:T(2,128)(2,1)} %param.1), channel_id=1, source_target_pairs={{0,3},{1,4},{2,5},{3,6},{4,7},{5,8},{6,9},{7,10},{8,11},{9,12},{10... | collective-permute-start | bytes 1572872 | tf_op jit(solution)/shard_map/ppermute | solution.py:15
  21.5 65.9 %copy-start = (bf16[128,2,1024]{2,1,0:T(2,128)(2,1)S(1)}, bf16[128,2,1024]{2,1,0:T(2,128)(2,1)}, u32[]{:S(2)}) copy-start(bf16[128,2,1024]{2,1,0:T(2,128)(2,1)} %param.1) | copy-start | bytes 1572868
  21.5 63.8 %collective-permute-start = (bf16[96,2,1024]{2,1,0:T(2,128)(2,1)}, bf16[96,2,1024]{2,1,0:T(2,128)(2,1)S(1)}, u32[]{:S(2)}, u32[]{:S(2)}) collective-permute-start(bf16[96,2,1024]{2,1,0:T(2,128)(2,1)} %slice.142), channel_id=1, source_target_pairs={{0,4},{1,5},{2,6},{3,7},{4,8},{5,9},{6,10},{7,11},{8,12},{9,13},{1... | collective-permute-start | bytes 1179656 | tf_op jit(solution)/shard_map/ppermute | solution.py:15
  87.8 9.2 %copy-start.1 = (f32[64,64,1]{1,0,2:T(8,128)S(1)}, f32[64,64,1]{1,0,2:T(8,128)}, u32[]{:S(2)}) copy-start(f32[64,64,1]{1,0,2:T(8,128)} %reshape.353) | copy-start | bytes 49156
Sparse Core Ops, SparseCore 0:
  172.3 65.2 all-gather.1
where the time goes:
time: 250 us; the launch traced here: 249 us
  waiting for transfers between devices  109 us (44%)
  blocking collectives  66 us (26%)
  local copies, waits for them, and re-layouts  23.9 us (10%)
  starting transfers between devices  19.2 us (8%)
  between operations  14.2 us (6%)
  other arithmetic  11.1 us (4%)
  matrix products  6.02 us (2%)
    all_gather x1, waiting for transfers between devices, per_device(): lax.all_gather(turned, 'tr', axis=3, tiled=True)  64.3 us
    all_to_all x1, blocking collectives, per_device(): lax.all_to_all(spectra, 'tr', split_axis=3, concat_axis=0, tiled=True)  47.8 us
    ppermute x4, waiting for transfers between devices, shifted(): return lax.ppermute(block, axis, route)  44.7 us
    ppermute x4, starting transfers between devices, shifted(): return lax.ppermute(block, axis, route)  19.2 us
    all_to_all x1, blocking collectives, per_device(): lax.all_to_all(lax.all_to_all(spectra, 'tr', split_axis=3, concat_axis=0,...  18.2 us
    add x1, other arithmetic, filterbank(): weighted + tap_table[tap_index][None, :, None, None] * extended[tap_index...  8.46 us
    mul x32, local copies, waits for them, and re-layouts, filterbank(): tap_table[tap_index][None, :, None, None]  7.99 us
  transfers between devices with their start and end apart: 5, of which 2 were waited for; matrix products, arithmetic and copies ran while one was open for 7% of the time, Pallas kernels for 0%

commit v1 on v0

v1 whole, which is shorter than its diff:
```python
import math

import jax
import jax.numpy as jnp
import ml_dtypes
import numpy as np
from jax import lax
from jax.experimental import pallas as pl
from jax.experimental.pallas import tpu as pltpu
from jax.sharding import PartitionSpec as P

MESH = pl.DeviceIdType.MESH
BF16 = jnp.bfloat16
F32 = jnp.float32

FINE = 32
TAPS = 16
LANES = 128
TC = 8
LINE = 4
CORES = 2
KK = FINE // TC
HOPS = 4
ROWS = HOPS * FINE * 2
OLD = 4
WINDOW = 6
HALF = 16
OFF = (0, 1, 7, 2, 6, 3, 5, 4)


def filter_constant():
    length = TAPS * FINE
    offset = (np.arange(length) - (length - 1) / 2.0) / FINE
    prototype = np.sin(math.pi * offset) / (math.pi * offset)
    taps = (prototype / np.sqrt(np.sum(prototype * prototype))).reshape(TAPS, FINE)
    index = np.arange(FINE)
    angle = 2.0 * math.pi * np.mod(index[:, None] * index[None, :], FINE) / FINE
    cosine, sine = np.cos(angle), np.sin(angle)
    fourier = np.zeros((FINE, 2, FINE, 2))
    fourier[:, 0, :, 0] = cosine
    fourier[:, 1, :, 0] = sine
    fourier[:, 0, :, 1] = -sine
    fourier[:, 1, :, 1] = cosine
    table = np.zeros((FINE, 2, 8, WINDOW * HOPS, FINE, 2))
    for s in range(8):
        for t in range(TAPS):
            table[:, :, s, s + 1 + t] = np.transpose(taps[t][:, None, None, None] * fourier, (2, 3, 0, 1))
    table = table.reshape(FINE * 2 * 8, WINDOW * ROWS).astype(np.float32)
    high = table.astype(ml_dtypes.bfloat16)
    low = (table - high.astype(np.float32)).astype(ml_dtypes.bfloat16)
    cut = FINE * 2 * 8 // 2
    return np.stack([np.concatenate([high[i * cut:(i + 1) * cut], low[i * cut:(i + 1) * cut]]) for i in range(2)])


def kernel(x_ref, g_hbm, out_ref, g_ref, raw, s_ref, r1, r0,
           g_sem, own_sem, ring_send, ring_recv, halo_send, halo_recv,
           turn1_send, turn1_recv, turn0_send, turn0_recv, own1_sem, own0_sem,
           line1_send, line1_recv, line0_send, line0_recv,
           pair1_send, pair1_recv, pair0_send, pair0_recv):
    tr = lax.axis_index("tr")
    y = lax.axis_index("tc")
    core = lax.rem(tr, 2)
    zl = tr // 2
    other = 1 - core
    sibling = zl * 2 + other

    table = pltpu.make_async_copy(g_hbm, g_ref, g_sem)
    table.start()

    def at(q, sign):
        return lax.rem(y + sign * OFF[q] + TC, TC)

    barrier = pltpu.get_barrier_semaphore()

    def greet(t, c):
        pl.semaphore_signal(barrier, inc=1, device_id={"tr": t, "tc": c}, device_id_type=MESH)

    for q in range(1, TC):
        greet(tr, at(q, -1))
    greet(sibling, y)

    @pl.when(zl > 0)
    def _():
        greet(tr - 2, y)

    @pl.when(zl < LINE - 1)
    def _():
        greet(tr + 2, y)

    @pl.when((core == 1) & (zl < LINE - 1))
    def _():
        greet(tr + 1, y)

    @pl.when((core == 0) & (zl > 0))
    def _():
        greet(tr - 1, y)

    inner = (zl > 0).astype(jnp.int32) + (zl < LINE - 1).astype(jnp.int32)
    halo_peer = jnp.where(core == 1, (zl < LINE - 1).astype(jnp.int32), (zl > 0).astype(jnp.int32))
    pl.semaphore_wait(barrier, TC + inner + halo_peer)

    def remote(src, dst, send, recv, t, c):
        return pltpu.make_async_remote_copy(
            src_ref=src, dst_ref=dst, send_sem=send, recv_sem=recv,
            device_id={"tr": t, "tc": c}, device_id_type=MESH)

    for q in range(TC - 1, 0, -1):
        c = at(q, -1)
        remote(x_ref.at[c], raw.at[OLD + y], ring_send, ring_recv, tr, c).start()
    own = pltpu.make_async_copy(x_ref.at[y], raw.at[OLD + y], own_sem)
    own.start()

    @pl.when(tr == 0)
    def _():
        raw[0:OLD] = jnp.zeros((OLD, ROWS, LANES), BF16)

    own.wait()
    arrivals = remote(x_ref.at[pl.ds(0, TC - 1)], raw.at[pl.ds(OLD, TC - 1)], ring_send, ring_recv, tr, y)
    arrivals.wait_recv()

    last = 2 * LINE - 1
    halo = remote(raw.at[pl.ds(TC, OLD)], raw.at[pl.ds(0, OLD)], halo_send, halo_recv, jnp.minimum(tr + 1, last), y)

    @pl.when(tr < last)
    def _():
        halo.start()

    table.wait()

    def filterbank(half):
        first = HOPS * half
        window = jnp.concatenate(
            [raw[first:first + WINDOW].reshape(WINDOW * ROWS, LANES),
             raw[first + 2:first + 2 + WINDOW].reshape(WINDOW * ROWS, LANES)], axis=1)
        for part in range(2):
            both = jnp.dot(g_ref[part], window, preferred_element_type=F32)
            count = both.shape[0] // 2
            total = both[:count] + both[count:]
            pair = jnp.concatenate(
                [total[:, :LANES].reshape(count // 8, 8, LANES), total[:, LANES:].reshape(count // 8, 8, LANES)],
                axis=1)
            s_ref[half, part * (TC // 2):(part + 1) * (TC // 2)] = pair.astype(BF16).reshape(
                TC // 2, KK, 2, HALF, LANES)

    filterbank(1)
    own1 = pltpu.make_async_copy(s_ref.at[1, y], r1.at[core, zl, y], own1_sem)
    own1.start()
    for q in range(1, TC):
        c = at(q, -1)
        remote(s_ref.at[1, c], r1.at[core, zl, y], turn1_send, turn1_recv.at[q], tr, c).start()

    def spread(r, s, piece, line_send, line_recv, pair_send, pair_recv, rightward, leftward):
        src = piece(r, s)
        if rightward:
            @pl.when(zl < LINE - 1)
            def _():
                remote(src, src, line_send.at[0, s], line_recv, jnp.minimum(tr + 2, last), y).start()
        if leftward:
            @pl.when(zl > 0)
            def _():
                remote(src, src, line_send.at[1, s], line_recv, jnp.maximum(tr - 2, 0), y).start()
        remote(src, src, pair_send.at[s], pair_recv, sibling, y).start()

    def piece1(q):
        return lambda r, s: r.at[core, s, at(q, 1)]

    def piece0(k):
        return lambda r, s: r.at[core, s, k]

    def from_line(i, dist, pieces, r, piece_of, line_send, line_recv, pair_send, pair_recv_of):
        p = i - dist
        if p < 0 or p >= pieces:
            return

        @pl.when(zl >= dist)
        def _():
            s = jnp.maximum(zl - dist, 0)
            piece = piece_of(p)
            remote(piece(r, s), piece(r, s), line_send.at[0, s], line_recv.at[s, p], sibling, y).wait_recv()
            spread(r, s, piece, line_send, line_recv.at[s, p], pair_send, pair_recv_of(s, p), True, False)

        @pl.when(zl < LINE - dist)
        def _():
            s = jnp.minimum(zl + dist, LINE - 1)
            piece = piece_of(p)
            remote(piece(r, s), piece(r, s), line_send.at[1, s], line_recv.at[s, p], sibling, y).wait_recv()
            spread(r, s, piece, line_send, line_recv.at[s, p], pair_send, pair_recv_of(s, p), False, True)

    def pair1_of(s, p):
        return pair1_recv

    def pair0_of(s, p):
        return pair0_recv.at[p]

    for i in range(TC + LINE - 1):
        if i < TC:
            piece = piece1(i)
            if i == 0:
                own1.wait()
            else:
                c = at(i, 1)
                remote(s_ref.at[1, 0], r1.at[core, zl, c], turn1_send, turn1_recv.at[i], sibling, y).wait_recv()
            spread(r1, zl, piece, line1_send, line1_recv.at[zl, i], pair1_send, pair1_recv, True, True)
        for dist in range(1, LINE):
            from_line(i, dist, TC, r1, piece1, line1_send, line1_recv, pair1_send, pair1_of)
        if i == 0:
            @pl.when(tr > 0)
            def _():
                halo.wait_recv()

            filterbank(0)
            own0 = pltpu.make_async_copy(s_ref.at[0, y], r0.at[core, zl, :, y], own0_sem)
            own0.start()
            for q in range(1, TC):
                c = at(q, -1)
                remote(s_ref.at[0, c], r0.at[core, zl, :, y], turn0_send, turn0_recv, tr, c).start()

    own0.wait()
    remote(r0.at[core, zl, :, pl.ds(0, TC - 1)], r0.at[core, zl, :, pl.ds(0, TC - 1)],
           turn0_send, turn0_recv, sibling, y).wait_recv()

    def correlate(k):
        def block(b):
            return jnp.concatenate(
                [r1[:, :, b, k].reshape(TC * 2 * HALF, LANES), r0[:, :, k, b].reshape(TC * 2 * HALF, LANES)], axis=0)

        mine = jnp.concatenate([r1[:, :, tr, k], r0[:, :, k, tr]], axis=0)
        swapped = jnp.concatenate([mine[:, :, 1:2], -mine[:, :, 0:1]], axis=2)
        depth = 2 * TC * 2 * HALF
        left = jnp.concatenate([mine.reshape(depth, LANES), swapped.reshape(depth, LANES)], axis=1)
        right = jnp.concatenate([block(b) for b in range(TC)], axis=1)
        product = lax.dot_general(left, right, (((0,), (0,)), ((), ())), preferred_element_type=F32)
        product = product * (1.0 / (LINE * CORES * 2 * HALF))
        out_ref[k] = product.astype(BF16).reshape(2, LANES, TC * LANES)

    def tail_waits():
        table_half = s_ref.at[1, pl.ds(0, TC - 1)]
        arrivals.wait_send()

        @pl.when(tr < last)
        def _():
            halo.wait_send()

        remote(table_half, table_half, turn1_send, turn1_recv.at[0], sibling, y).wait_send()
        remote(table_half, table_half, turn0_send, turn0_recv, sibling, y).wait_send()
        sent_waits(r1, line1_send, pair1_send)
        remote(r1.at[other], r1.at[other], pair1_send.at[0], pair1_recv, sibling, y).wait_recv()

    def sent_waits(r, line_send, pair_send):
        for s in range(LINE):
            whole = r.at[core, s]

            @pl.when((zl < LINE - 1) & (s <= zl))
            def _():
                remote(whole, whole, line_send.at[0, s], pair0_recv.at[0], sibling, y).wait_send()

            @pl.when((zl > 0) & (s >= zl))
            def _():
                remote(whole, whole, line_send.at[1, s], pair0_recv.at[0], sibling, y).wait_send()

            remote(whole, whole, pair_send.at[s], pair0_recv.at[0], sibling, y).wait_send()

    for i in range(KK + LINE - 1):
        if i < KK:
            spread(r0, zl, piece0(i), line0_send, line0_recv.at[zl, i], pair0_send, pair0_recv.at[i], True, True)
        if i == KK - 1:
            tail_waits()
        for dist in range(1, LINE):
            from_line(i, dist, KK, r0, piece0, line0_send, line0_recv, pair0_send, pair0_of)
        k = i - (LINE - 1)
        if k >= 0:
            theirs = r0.at[other, :, k]
            remote(theirs, theirs, pair0_send.at[0], pair0_recv.at[k], sibling, y).wait_recv()
            correlate(k)
    sent_waits(r0, line0_send, pair0_send)


def per_device(voltages):
    samples, _, inputs = voltages.shape
    blocks = inputs // LANES
    x = voltages.reshape(samples, 2, blocks, LANES).transpose(2, 0, 1, 3).reshape(blocks, samples * 2, LANES)
    table = jnp.asarray(filter_constant())
    any_spec = pl.BlockSpec(memory_space=pl.ANY)
    dma = pltpu.SemaphoreType.DMA
    return pl.pallas_call(
        kernel,
        out_shape=jax.ShapeDtypeStruct((KK, 2, LANES, inputs), BF16),
        in_specs=[any_spec, pl.BlockSpec(memory_space=pltpu.HBM)],
        out_specs=pl.BlockSpec(memory_space=pltpu.VMEM),
        scratch_shapes=[
            pltpu.VMEM(table.shape, BF16),
            pltpu.VMEM((OLD + TC, ROWS, LANES), BF16),
            pltpu.VMEM((2, TC, KK, 2, HALF, LANES), BF16),
            pltpu.VMEM((CORES, LINE, TC, KK, 2, HALF, LANES), BF16),
            pltpu.VMEM((CORES, LINE, KK, TC, 2, HALF, LANES), BF16),
            dma, dma, dma, dma, dma, dma,
            dma, dma((TC,)), dma, dma, dma, dma,
            dma((2, LINE)), dma((LINE, TC)), dma((2, LINE)), dma((LINE, KK)),
            dma((LINE,)), dma, dma((LINE,)), dma((KK,)),
        ],
        compiler_params=pltpu.CompilerParams(
            collective_id=0, has_side_effects=True, vmem_limit_bytes=51 * 1024 * 1024),
    )(x, table)


def solution(mesh):
    return jax.shard_map(
        per_device,
        mesh=mesh,
        in_specs=(P(("band", "tr", "tc"), None, None),),
        out_specs=P(("band", "tc"), None, "tr", None),
        check_vma=False,
    )
```

time: 250 us -> 75.1 us (0.30)
  waiting for transfers between devices: 109 us -> 0 us
  Pallas kernels: 0 us -> 71.7 us
  blocking collectives: 66 us -> 0 us
  local copies, waits for them, and re-layouts: 23.9 us -> 2.72 us
  starting transfers between devices: 19.2 us -> 0 us
  between operations: 14.2 us -> 0.01 us
  other arithmetic: 11.1 us -> 0 us
  matrix products: 6.02 us -> 0 us
    pallas_call x0 -> x1, Pallas kernels: none -> 71.7 us  [per_device(): pl.pallas_call(kernel, out_shape=jax.ShapeDtypeStruct((KK, 2, LANES, inpu...]
    all_to_all x2 -> x0, blocking collectives: 66 us -> none  [the longest x1 47.8 us: per_device(): lax.all_to_all(spectra, 'tr', split_axis=3, concat_axis=0, tiled=True)]
    all_gather x1 -> x0, waiting for transfers between devices: 64.3 us -> none  [per_device(): lax.all_gather(turned, 'tr', axis=3, tiled=True)]
    ppermute x4 -> x0, waiting for transfers between devices: 44.7 us -> none  [shifted(): return lax.ppermute(block, axis, route)]
    ppermute x4 -> x0, starting transfers between devices: 19.2 us -> none  [shifted(): return lax.ppermute(block, axis, route)]
    add x1 -> x0, other arithmetic: 8.46 us -> none  [filterbank(): weighted + tap_table[tap_index][None, :, None, None] * extended[tap_index...]
    mul x32 -> x0, local copies, waits for them, and re-layouts: 7.99 us -> none  [filterbank(): tap_table[tap_index][None, :, None, None]]
    dot_general x2 -> x0, matrix products: 6.02 us -> none  [the longest x1 4.98 us: per_device(): jnp.einsum('rskci,skcj->krij', stacked, lax.all_gather(turned, 'tr', axis...]
  transfers between devices with their start and end apart: 5 -> 0, of which waited for: 2 -> 0; matrix products, arithmetic and copies ran while one was open for 7% -> 0% of each run, Pallas kernels for 0% -> 0%
where the time goes in v1:
time: 75.1 us; the launch traced here: 74.5 us
  Pallas kernels  71.7 us (95%)
  local copies, waits for them, and re-layouts  2.72 us (4%)
    pallas_call x1, Pallas kernels, per_device(): pl.pallas_call(kernel, out_shape=jax.ShapeDtypeStruct((KK, 2, LANES, inpu...  71.7 us
    unnamed x3, local copies, waits for them, and re-layouts  2.36 us

profile of v1, /device:TPU:1, one launch (start us, length us, event | category | flops | bytes accessed | tf_op | source)
XLA Modules:
  0.0 74.5 jit_solution(8548868631317748717)
XLA Ops:
  0.0 0.0 copy-start
  0.0 1.0 %copy-done = bf16[128,2,1024]{2,1,0:T(2,128)(2,1)S(1)} copy-done((bf16[128,2,1024]{2,1,0:T(2,128)(2,1)S(1)}, bf16[128,2,1024]{2,1,0:T(2,128)(2,1)}, u32[]{:S(2)}) %copy-start) | copy-done | bytes 524312
  1.0 0.4 copy_bitcast_fusion
  1.4 71.7 %shard_map.28 = bf16[4,2,128,1024]{3,2,1,0:T(8,128)(2,1)S(1)} custom-call(bf16[8,256,128]{2,1,0:T(8,128)(2,1)S(1)} %bitcast.8, bf16[2,512,1536]{2,1,0:T(8,128)(2,1)} %constant.2.clone.g_hbm), custom_call_target="tpu_custom_call" | custom-call | tf_op jit(solution)/shard_map/pallas_call | solution.py:285
  73.1 1.3 %copy.7 = bf16[4,2,128,1024]{3,2,1,0:T(8,128)(2,1)} copy(bf16[4,2,128,1024]{3,2,1,0:T(8,128)(2,1)S(1)} %shard_map.28) | data formatting | bytes 4194304
Async XLA Ops:
  0.0 1.0 %copy-start = (bf16[128,2,1024]{2,1,0:T(2,128)(2,1)S(1)}, bf16[128,2,1024]{2,1,0:T(2,128)(2,1)}, u32[]{:S(2)}) copy-start(bf16[128,2,1024]{2,1,0:T(2,128)(2,1)} %param.2) | copy-start | bytes 1572868

commit v2 on v1

--- a/solution.py
+++ b/solution.py
@@ -25,7 +25,11 @@
 OLD = 4
 WINDOW = 6
 HALF = 16
+PART = 4
 OFF = (0, 1, 7, 2, 6, 3, 5, 4)
+UNITS = TC + KK
+LAG = (2, 4, 6)
+ORDER = ((0, 0), (TC - 1, 2))
 
 
 def filter_constant():
@@ -48,15 +52,15 @@
     table = table.reshape(FINE * 2 * 8, WINDOW * ROWS).astype(np.float32)
     high = table.astype(ml_dtypes.bfloat16)
     low = (table - high.astype(np.float32)).astype(ml_dtypes.bfloat16)
-    cut = FINE * 2 * 8 // 2
-    return np.stack([np.concatenate([high[i * cut:(i + 1) * cut], low[i * cut:(i + 1) * cut]]) for i in range(2)])
+    return np.concatenate([high.reshape(TC, -1, WINDOW * ROWS), low.reshape(TC, -1, WINDOW * ROWS)], axis=1)
 
 
 def kernel(x_ref, g_hbm, out_ref, g_ref, raw, s_ref, r1, r0,
            g_sem, own_sem, ring_send, ring_recv, halo_send, halo_recv,
            turn1_send, turn1_recv, turn0_send, turn0_recv, own1_sem, own0_sem,
            line1_send, line1_recv, line0_send, line0_recv,
-           pair1_send, pair1_recv, pair0_send, pair0_recv):
+           pair1_send, pair1_recv, pair0_send, pair0_recv,
+           line_ok, pair_ok, halo_ok):
     tr = lax.axis_index("tr")
     y = lax.axis_index("tc")
     core = lax.rem(tr, 2)
@@ -77,27 +81,45 @@
 
     for q in range(1, TC):
         greet(tr, at(q, -1))
-    greet(sibling, y)
-
-    @pl.when(zl > 0)
-    def _():
-        greet(tr - 2, y)
-
-    @pl.when(zl < LINE - 1)
-    def _():
-        greet(tr + 2, y)
-
-    @pl.when((core == 1) & (zl < LINE - 1))
-    def _():
-        greet(tr + 1, y)
-
-    @pl.when((core == 0) & (zl > 0))
-    def _():
-        greet(tr - 1, y)
-
-    inner = (zl > 0).astype(jnp.int32) + (zl < LINE - 1).astype(jnp.int32)
-    halo_peer = jnp.where(core == 1, (zl < LINE - 1).astype(jnp.int32), (zl > 0).astype(jnp.int32))
-    pl.semaphore_wait(barrier, TC + inner + halo_peer)
+    last = 2 * LINE - 1
+    below = (zl > 0).astype(jnp.int32)
+    above = (zl < LINE - 1).astype(jnp.int32)
+
+    @pl.when(core == 1)
+    def _():
+        @pl.when(zl < LINE - 1)
+        def _():
+            greet(jnp.minimum(tr + 2, last), y)
+            greet(jnp.minimum(tr + 1, last), y)
+
+    @pl.when(core == 0)
+    def _():
+        @pl.when(zl > 0)
+        def _():
+            greet(jnp.maximum(tr - 2, 0), y)
+
+    pl.semaphore_wait(barrier, TC - 1 + jnp.where(core == 1, below, 1 + above + below))
+
+    def tell(sem, t):
+        pl.semaphore_signal(sem, inc=1, device_id={"tr": t, "tc": y}, device_id_type=MESH)
+
+    @pl.when(core == 1)
+    def _():
+        @pl.when(zl > 0)
+        def _():
+            tell(line_ok, jnp.maximum(tr - 2, 0))
+
+    @pl.when(core == 0)
+    def _():
+        tell(pair_ok, sibling)
+
+        @pl.when(zl > 0)
+        def _():
+            tell(halo_ok, jnp.maximum(tr - 1, 0))
+
+        @pl.when(zl < LINE - 1)
+        def _():
+            tell(line_ok, jnp.minimum(tr + 2, last))
 
     def remote(src, dst, send, recv, t, c):
         return pltpu.make_async_remote_copy(
@@ -116,38 +138,52 @@
 
     own.wait()
     arrivals = remote(x_ref.at[pl.ds(0, TC - 1)], raw.at[pl.ds(OLD, TC - 1)], ring_send, ring_recv, tr, y)
+    arrivals.wait_send()
+
+    @pl.when(core == 1)
+    def _():
+        greet(sibling, y)
+
     arrivals.wait_recv()
 
-    last = 2 * LINE - 1
     halo = remote(raw.at[pl.ds(TC, OLD)], raw.at[pl.ds(0, OLD)], halo_send, halo_recv, jnp.minimum(tr + 1, last), y)
 
+    @pl.when((core == 1) & (tr < last))
+    def _():
+        pl.semaphore_wait(halo_ok, 1)
+
     @pl.when(tr < last)
     def _():
         halo.start()
 
     table.wait()
 
-    def filterbank(half):
+    def filterbank(half, after):
         first = HOPS * half
         window = jnp.concatenate(
             [raw[first:first + WINDOW].reshape(WINDOW * ROWS, LANES),
              raw[first + 2:first + 2 + WINDOW].reshape(WINDOW * ROWS, LANES)], axis=1)
         for part in range(2):
-            both = jnp.dot(g_ref[part], window, preferred_element_type=F32)
-            count = both.shape[0] // 2
-            total = both[:count] + both[count:]
-            pair = jnp.concatenate(
-                [total[:, :LANES].reshape(count // 8, 8, LANES), total[:, LANES:].reshape(count // 8, 8, LANES)],
-                axis=1)
-            s_ref[half, part * (TC // 2):(part + 1) * (TC // 2)] = pair.astype(BF16).reshape(
-                TC // 2, KK, 2, HALF, LANES)
-
-    filterbank(1)
+            groups = [at(q, -1) for q in range(part * PART, (part + 1) * PART)]
+            both = jnp.dot(jnp.concatenate([g_ref[c] for c in groups], axis=0), window, preferred_element_type=F32)
+            both = both.reshape(PART, 2, KK * 2, 8, 2 * LANES)
+            total = both[:, 0] + both[:, 1]
+            pair = jnp.concatenate([total[..., :LANES], total[..., LANES:]], axis=2).astype(BF16)
+            for j, c in enumerate(groups):
+                s_ref[half, c] = pair[j].reshape(KK, 2, HALF, LANES)
+            after(part)
+
     own1 = pltpu.make_async_copy(s_ref.at[1, y], r1.at[core, zl, y], own1_sem)
-    own1.start()
-    for q in range(1, TC):
-        c = at(q, -1)
-        remote(s_ref.at[1, c], r1.at[core, zl, y], turn1_send, turn1_recv.at[q], tr, c).start()
+
+    def turn_second(part):
+        for q in range(part * PART, (part + 1) * PART):
+            if q == 0:
+                own1.start()
+            else:
+                c = at(q, -1)
+                remote(s_ref.at[1, c], r1.at[core, zl, y], turn1_send, turn1_recv.at[q], tr, c).start()
+
+    filterbank(1, turn_second)
 
     def spread(r, s, piece, line_send, line_recv, pair_send, pair_recv, rightward, leftward):
         src = piece(r, s)
@@ -167,11 +203,7 @@
     def piece0(k):
         return lambda r, s: r.at[core, s, k]
 
-    def from_line(i, dist, pieces, r, piece_of, line_send, line_recv, pair_send, pair_recv_of):
-        p = i - dist
-        if p < 0 or p >= pieces:
-            return
-
+    def from_line(dist, p, r, piece_of, line_send, line_recv, pair_send, pair_recv_of):
         @pl.when(zl >= dist)
         def _():
             s = jnp.maximum(zl - dist, 0)
@@ -192,32 +224,19 @@
     def pair0_of(s, p):
         return pair0_recv.at[p]
 
-    for i in range(TC + LINE - 1):
-        if i < TC:
-            piece = piece1(i)
-            if i == 0:
-                own1.wait()
-            else:
-                c = at(i, 1)
-                remote(s_ref.at[1, 0], r1.at[core, zl, c], turn1_send, turn1_recv.at[i], sibling, y).wait_recv()
-            spread(r1, zl, piece, line1_send, line1_recv.at[zl, i], pair1_send, pair1_recv, True, True)
-        for dist in range(1, LINE):
-            from_line(i, dist, TC, r1, piece1, line1_send, line1_recv, pair1_send, pair1_of)
-        if i == 0:
-            @pl.when(tr > 0)
-            def _():
-                halo.wait_recv()
-
-            filterbank(0)
-            own0 = pltpu.make_async_copy(s_ref.at[0, y], r0.at[core, zl, :, y], own0_sem)
-            own0.start()
+    def first_half():
+        @pl.when(tr > 0)
+        def _():
+            halo.wait_recv()
+
+        filterbank(0, lambda part: None)
+        own0.start()
+        for k in range(KK):
             for q in range(1, TC):
                 c = at(q, -1)
-                remote(s_ref.at[0, c], r0.at[core, zl, :, y], turn0_send, turn0_recv, tr, c).start()
-
-    own0.wait()
-    remote(r0.at[core, zl, :, pl.ds(0, TC - 1)], r0.at[core, zl, :, pl.ds(0, TC - 1)],
-           turn0_send, turn0_recv, sibling, y).wait_recv()
+                remote(s_ref.at[0, c, k], r0.at[core, zl, k, y], turn0_send, turn0_recv.at[k], tr, c).start()
+
+    own0 = pltpu.make_async_copy(s_ref.at[0, y], r0.at[core, zl, :, y], own0_sem)
 
     def correlate(k):
         def block(b):
@@ -235,14 +254,12 @@
 
     def tail_waits():
         table_half = s_ref.at[1, pl.ds(0, TC - 1)]
-        arrivals.wait_send()
-
         @pl.when(tr < last)
         def _():
             halo.wait_send()
 
         remote(table_half, table_half, turn1_send, turn1_recv.at[0], sibling, y).wait_send()
-        remote(table_half, table_half, turn0_send, turn0_recv, sibling, y).wait_send()
+        remote(table_half, table_half, turn0_send, turn0_recv.at[0], sibling, y).wait_send()
         sent_waits(r1, line1_send, pair1_send)
         remote(r1.at[other], r1.at[other], pair1_send.at[0], pair1_recv, sibling, y).wait_recv()
 
@@ -260,18 +277,64 @@
 
             remote(whole, whole, pair_send.at[s], pair0_recv.at[0], sibling, y).wait_send()
 
-    for i in range(KK + LINE - 1):
-        if i < KK:
-            spread(r0, zl, piece0(i), line0_send, line0_recv.at[zl, i], pair0_send, pair0_recv.at[i], True, True)
-        if i == KK - 1:
-            tail_waits()
-        for dist in range(1, LINE):
-            from_line(i, dist, KK, r0, piece0, line0_send, line0_recv, pair0_send, pair0_of)
-        k = i - (LINE - 1)
-        if k >= 0:
-            theirs = r0.at[other, :, k]
-            remote(theirs, theirs, pair0_send.at[0], pair0_recv.at[k], sibling, y).wait_recv()
-            correlate(k)
+    def take_own(u):
+        if u < TC:
+            if u == 0:
+                own1.wait()
+            else:
+                c = at(u, 1)
+                remote(s_ref.at[1, 0], r1.at[core, zl, c], turn1_send, turn1_recv.at[u], sibling, y).wait_recv()
+            spread(r1, zl, piece1(u), line1_send, line1_recv.at[zl, u], pair1_send, pair1_recv, True, True)
+            return
+        k = u - TC
+        if k == 0:
+            own0.wait()
+        seven = r0.at[core, zl, k, pl.ds(0, TC - 1)]
+        remote(seven, seven, turn0_send, turn0_recv.at[k], sibling, y).wait_recv()
+        spread(r0, zl, piece0(k), line0_send, line0_recv.at[zl, k], pair0_send, pair0_recv.at[k], True, True)
+
+    def take_line(dist, u):
+        if u < TC:
+            from_line(dist, u, r1, piece1, line1_send, line1_recv, pair1_send, pair1_of)
+        else:
+            from_line(dist, u - TC, r0, piece0, line0_send, line0_recv, pair0_send, pair0_of)
+
+    @pl.when(((core == 1) & (zl < LINE - 1)) | ((core == 0) & (zl > 0)))
+    def _():
+        pl.semaphore_wait(line_ok, 1)
+
+    @pl.when(core == 1)
+    def _():
+        pl.semaphore_wait(pair_ok, 1)
+
+    def run(first_at, gap):
+        place = [u if u < TC else u + gap for u in range(UNITS)]
+        for i in range(place[-1] + LAG[2] + 1):
+            for u in range(UNITS):
+                if place[u] == i:
+                    take_own(u)
+            if i == first_at:
+                first_half()
+            for dist in range(1, LINE):
+                for u in range(UNITS):
+                    if place[u] + LAG[dist - 1] == i:
+                        take_line(dist, u)
+            for k in range(KK):
+                if place[TC + k] + LAG[2] == i:
+                    if k == 0:
+                        tail_waits()
+                    theirs = r0.at[other, :, k]
+                    remote(theirs, theirs, pair0_send.at[0], pair0_recv.at[k], sibling, y).wait_recv()
+                    correlate(k)
+
+    @pl.when(core == 1)
+    def _():
+        run(*ORDER[1])
+
+    @pl.when(core == 0)
+    def _():
+        run(*ORDER[0])
+
     sent_waits(r0, line0_send, pair0_send)
 
 
@@ -294,9 +357,10 @@
             pltpu.VMEM((CORES, LINE, TC, KK, 2, HALF, LANES), BF16),
             pltpu.VMEM((CORES, LINE, KK, TC, 2, HALF, LANES), BF16),
             dma, dma, dma, dma, dma, dma,
-            dma, dma((TC,)), dma, dma, dma, dma,
+            dma, dma((TC,)), dma, dma((KK,)), dma, dma,
             dma((2, LINE)), dma((LINE, TC)), dma((2, LINE)), dma((LINE, KK)),
             dma((LINE,)), dma, dma((LINE,)), dma((KK,)),
+            pltpu.SemaphoreType.REGULAR, pltpu.SemaphoreType.REGULAR, pltpu.SemaphoreType.REGULAR,
         ],
         compiler_params=pltpu.CompilerParams(
             collective_id=0, has_side_effects=True, vmem_limit_bytes=51 * 1024 * 1024),

time: 75.1 us -> 68.6 us (0.913)
  Pallas kernels: 71.7 us -> 65.7 us
    pallas_call x1, Pallas kernels: 71.7 us -> 65.7 us  [per_device(): pl.pallas_call(kernel, out_shape=jax.ShapeDtypeStruct((KK, 2, LANES, inpu...]
where the time goes in v2:
time: 68.6 us; the launch traced here: 68.4 us
  Pallas kernels  65.7 us (96%)
  local copies, waits for them, and re-layouts  2.72 us (4%)
    pallas_call x1, Pallas kernels, per_device(): pl.pallas_call(kernel, out_shape=jax.ShapeDtypeStruct((KK, 2, LANES, inpu...  65.7 us
    unnamed x3, local copies, waits for them, and re-layouts  2.36 us

profile of v2, /device:TPU:1, one launch (start us, length us, event | category | flops | bytes accessed | tf_op | source)
XLA Modules:
  0.0 68.4 jit_solution(4738539450611707014)
XLA Ops:
  0.0 0.0 copy-start
  0.0 1.0 %copy-done = bf16[128,2,1024]{2,1,0:T(2,128)(2,1)S(1)} copy-done((bf16[128,2,1024]{2,1,0:T(2,128)(2,1)S(1)}, bf16[128,2,1024]{2,1,0:T(2,128)(2,1)}, u32[]{:S(2)}) %copy-start) | copy-done | bytes 524312
  1.0 0.4 copy_bitcast_fusion
  1.4 65.7 %shard_map.28 = bf16[4,2,128,1024]{3,2,1,0:T(8,128)(2,1)S(1)} custom-call(bf16[8,256,128]{2,1,0:T(8,128)(2,1)S(1)} %bitcast.8, bf16[8,128,1536]{2,1,0:T(8,128)(2,1)} %constant.2.clone.g_hbm), custom_call_target="tpu_custom_call" | custom-call | tf_op jit(solution)/shard_map/pallas_call | solution.py:348
  67.1 1.3 %copy.7 = bf16[4,2,128,1024]{3,2,1,0:T(8,128)(2,1)} copy(bf16[4,2,128,1024]{3,2,1,0:T(8,128)(2,1)S(1)} %shard_map.28) | data formatting | bytes 4194304
Async XLA Ops:
  0.0 1.0 %copy-start = (bf16[128,2,1024]{2,1,0:T(2,128)(2,1)S(1)}, bf16[128,2,1024]{2,1,0:T(2,128)(2,1)}, u32[]{:S(2)}) copy-start(bf16[128,2,1024]{2,1,0:T(2,128)(2,1)} %param.2) | copy-start | bytes 1572868

commit v3 on v2

--- a/solution.py
+++ b/solution.py
@@ -28,8 +28,7 @@
 PART = 4
 OFF = (0, 1, 7, 2, 6, 3, 5, 4)
 UNITS = TC + KK
-LAG = (2, 4, 6)
-ORDER = ((0, 0), (TC - 1, 2))
+ORDER = ((7, 2, (3, 6, 9)), (7, 2, (3, 6, 9)))
 
 
 def filter_constant():
@@ -55,7 +54,7 @@
     return np.concatenate([high.reshape(TC, -1, WINDOW * ROWS), low.reshape(TC, -1, WINDOW * ROWS)], axis=1)
 
 
-def kernel(x_ref, g_hbm, out_ref, g_ref, raw, s_ref, r1, r0,
+def kernel(x_ref, g_hbm, out_ref, g_ref, raw, s_ref, r1, r0, acc,
            g_sem, own_sem, ring_send, ring_recv, halo_send, halo_recv,
            turn1_send, turn1_recv, turn0_send, turn0_recv, own1_sem, own0_sem,
            line1_send, line1_recv, line0_send, line0_recv,
@@ -238,19 +237,23 @@
 
     own0 = pltpu.make_async_copy(s_ref.at[0, y], r0.at[core, zl, :, y], own0_sem)
 
+    def correlation(mine, block):
+        swapped = jnp.concatenate([mine[:, :, 1:2], -mine[:, :, 0:1]], axis=2)
+        depth = TC * 2 * HALF
+        left = jnp.concatenate([mine.reshape(depth, LANES), swapped.reshape(depth, LANES)], axis=1)
+        right = jnp.concatenate([block(b).reshape(depth, LANES) for b in range(TC)], axis=1)
+        return lax.dot_general(left, right, (((0,), (0,)), ((), ())), preferred_element_type=F32)
+
+    def second(k):
+        return correlation(r1[:, :, tr, k], lambda b: r1[:, :, b, k])
+
     def correlate(k):
-        def block(b):
-            return jnp.concatenate(
-                [r1[:, :, b, k].reshape(TC * 2 * HALF, LANES), r0[:, :, k, b].reshape(TC * 2 * HALF, LANES)], axis=0)
-
-        mine = jnp.concatenate([r1[:, :, tr, k], r0[:, :, k, tr]], axis=0)
-        swapped = jnp.concatenate([mine[:, :, 1:2], -mine[:, :, 0:1]], axis=2)
-        depth = 2 * TC * 2 * HALF
-        left = jnp.concatenate([mine.reshape(depth, LANES), swapped.reshape(depth, LANES)], axis=1)
-        right = jnp.concatenate([block(b) for b in range(TC)], axis=1)
-        product = lax.dot_general(left, right, (((0,), (0,)), ((), ())), preferred_element_type=F32)
+        product = acc[...] if k == KK - 1 else second(k)
+        product = product + correlation(r0[:, :, k, tr], lambda b: r0[:, :, k, b])
         product = product * (1.0 / (LINE * CORES * 2 * HALF))
         out_ref[k] = product.astype(BF16).reshape(2, LANES, TC * LANES)
+        if k == KK - 2:
+            acc[...] = second(KK - 1)
 
     def tail_waits():
         table_half = s_ref.at[1, pl.ds(0, TC - 1)]
@@ -307,9 +310,9 @@
     def _():
         pl.semaphore_wait(pair_ok, 1)
 
-    def run(first_at, gap):
+    def run(first_at, gap, lag):
         place = [u if u < TC else u + gap for u in range(UNITS)]
-        for i in range(place[-1] + LAG[2] + 1):
+        for i in range(place[-1] + lag[2] + 1):
             for u in range(UNITS):
                 if place[u] == i:
                     take_own(u)
@@ -317,10 +320,10 @@
                 first_half()
             for dist in range(1, LINE):
                 for u in range(UNITS):
-                    if place[u] + LAG[dist - 1] == i:
+                    if place[u] + lag[dist - 1] == i:
                         take_line(dist, u)
             for k in range(KK):
-                if place[TC + k] + LAG[2] == i:
+                if place[TC + k] + lag[2] == i:
                     if k == 0:
                         tail_waits()
                     theirs = r0.at[other, :, k]
@@ -356,6 +359,7 @@
             pltpu.VMEM((2, TC, KK, 2, HALF, LANES), BF16),
             pltpu.VMEM((CORES, LINE, TC, KK, 2, HALF, LANES), BF16),
             pltpu.VMEM((CORES, LINE, KK, TC, 2, HALF, LANES), BF16),
+            pltpu.VMEM((2 * LANES, inputs), F32),
             dma, dma, dma, dma, dma, dma,
             dma, dma((TC,)), dma, dma((KK,)), dma, dma,
             dma((2, LINE)), dma((LINE, TC)), dma((2, LINE)), dma((LINE, KK)),

time: 68.6 us -> 67.9 us (0.990)
  Pallas kernels: 65.7 us -> 65 us
    pallas_call x1, Pallas kernels: 65.7 us -> 65 us  [per_device(): pl.pallas_call(kernel, out_shape=jax.ShapeDtypeStruct((KK, 2, LANES, inpu...]
where the time goes in v3:
time: 67.9 us; the launch traced here: 67.7 us
  Pallas kernels  65 us (96%)
  local copies, waits for them, and re-layouts  2.72 us (4%)
    pallas_call x1, Pallas kernels, per_device(): pl.pallas_call(kernel, out_shape=jax.ShapeDtypeStruct((KK, 2, LANES, inpu...  65 us
    unnamed x3, local copies, waits for them, and re-layouts  2.36 us

profile of v3, /device:TPU:1, one launch (start us, length us, event | category | flops | bytes accessed | tf_op | source)
XLA Modules:
  0.0 67.7 jit_solution(15916322131063040383)
XLA Ops:
  0.0 0.0 copy-start
  0.0 1.0 %copy-done = bf16[128,2,1024]{2,1,0:T(2,128)(2,1)S(1)} copy-done((bf16[128,2,1024]{2,1,0:T(2,128)(2,1)S(1)}, bf16[128,2,1024]{2,1,0:T(2,128)(2,1)}, u32[]{:S(2)}) %copy-start) | copy-done | bytes 524312
  1.0 0.4 copy_bitcast_fusion
  1.4 65.0 %shard_map.28 = bf16[4,2,128,1024]{3,2,1,0:T(8,128)(2,1)S(1)} custom-call(bf16[8,256,128]{2,1,0:T(8,128)(2,1)S(1)} %bitcast.8, bf16[8,128,1536]{2,1,0:T(8,128)(2,1)} %constant.2.clone.g_hbm), custom_call_target="tpu_custom_call" | custom-call | tf_op jit(solution)/shard_map/pallas_call | solution.py:351
  66.4 1.3 %copy.7 = bf16[4,2,128,1024]{3,2,1,0:T(8,128)(2,1)} copy(bf16[4,2,128,1024]{3,2,1,0:T(8,128)(2,1)S(1)} %shard_map.28) | data formatting | bytes 4194304
Async XLA Ops:
  0.0 1.0 %copy-start = (bf16[128,2,1024]{2,1,0:T(2,128)(2,1)S(1)}, bf16[128,2,1024]{2,1,0:T(2,128)(2,1)}, u32[]{:S(2)}) copy-start(bf16[128,2,1024]{2,1,0:T(2,128)(2,1)} %param.2) | copy-start | bytes 1572868

commit v4 on v3

--- a/solution.py
+++ b/solution.py
@@ -28,7 +28,7 @@
 PART = 4
 OFF = (0, 1, 7, 2, 6, 3, 5, 4)
 UNITS = TC + KK
-ORDER = ((7, 2, (3, 6, 9)), (7, 2, (3, 6, 9)))
+ORDER = ((4, 2, (3, 6, 9)), (7, 4, (2, 4, 6)))
 
 
 def filter_constant():

time: 67.9 us -> 69 us (1.016)
  Pallas kernels: 65 us -> 66.1 us
    pallas_call x1, Pallas kernels: 65 us -> 66.1 us  [per_device(): pl.pallas_call(kernel, out_shape=jax.ShapeDtypeStruct((KK, 2, LANES, inpu...]
where the time goes in v4:
time: 69 us; the launch traced here: 68.9 us
  Pallas kernels  66.1 us (96%)
  local copies, waits for them, and re-layouts  2.72 us (4%)
    pallas_call x1, Pallas kernels, per_device(): pl.pallas_call(kernel, out_shape=jax.ShapeDtypeStruct((KK, 2, LANES, inpu...  66.1 us
    unnamed x3, local copies, waits for them, and re-layouts  2.36 us

profile of v4, /device:TPU:1, one launch (start us, length us, event | category | flops | bytes accessed | tf_op | source)
XLA Modules:
  0.0 68.9 jit_solution(16502784421764296723)
XLA Ops:
  0.0 0.0 copy-start
  0.0 1.0 %copy-done = bf16[128,2,1024]{2,1,0:T(2,128)(2,1)S(1)} copy-done((bf16[128,2,1024]{2,1,0:T(2,128)(2,1)S(1)}, bf16[128,2,1024]{2,1,0:T(2,128)(2,1)}, u32[]{:S(2)}) %copy-start) | copy-done | bytes 524312
  1.0 0.4 copy_bitcast_fusion
  1.4 66.1 %shard_map.28 = bf16[4,2,128,1024]{3,2,1,0:T(8,128)(2,1)S(1)} custom-call(bf16[8,256,128]{2,1,0:T(8,128)(2,1)S(1)} %bitcast.8, bf16[8,128,1536]{2,1,0:T(8,128)(2,1)} %constant.2.clone.g_hbm), custom_call_target="tpu_custom_call" | custom-call | tf_op jit(solution)/shard_map/pallas_call | solution.py:351
  67.5 1.3 %copy.7 = bf16[4,2,128,1024]{3,2,1,0:T(8,128)(2,1)} copy(bf16[4,2,128,1024]{3,2,1,0:T(8,128)(2,1)S(1)} %shard_map.28) | data formatting | bytes 4194304
Async XLA Ops:
  0.0 1.0 %copy-start = (bf16[128,2,1024]{2,1,0:T(2,128)(2,1)S(1)}, bf16[128,2,1024]{2,1,0:T(2,128)(2,1)}, u32[]{:S(2)}) copy-start(bf16[128,2,1024]{2,1,0:T(2,128)(2,1)} %param.2) | copy-start | bytes 1572868

commit v5 on v4

--- a/solution.py
+++ b/solution.py
@@ -28,7 +28,7 @@
 PART = 4
 OFF = (0, 1, 7, 2, 6, 3, 5, 4)
 UNITS = TC + KK
-ORDER = ((4, 2, (3, 6, 9)), (7, 4, (2, 4, 6)))
+ORDER = ((7, 0, (3, 6, 9)), (7, 2, (3, 6, 9)))
 
 
 def filter_constant():

time: 69 us -> 67.9 us (0.984)
  Pallas kernels: 66.1 us -> 65 us
    pallas_call x1, Pallas kernels: 66.1 us -> 65 us  [per_device(): pl.pallas_call(kernel, out_shape=jax.ShapeDtypeStruct((KK, 2, LANES, inpu...]
where the time goes in v5:
time: 67.9 us; the launch traced here: 67.7 us
  Pallas kernels  65 us (96%)
  local copies, waits for them, and re-layouts  2.72 us (4%)
    pallas_call x1, Pallas kernels, per_device(): pl.pallas_call(kernel, out_shape=jax.ShapeDtypeStruct((KK, 2, LANES, inpu...  65 us
    unnamed x3, local copies, waits for them, and re-layouts  2.36 us

profile of v5, /device:TPU:1, one launch (start us, length us, event | category | flops | bytes accessed | tf_op | source)
XLA Modules:
  0.0 67.7 jit_solution(7578266341718989970)
XLA Ops:
  0.0 0.0 copy-start
  0.0 1.0 %copy-done = bf16[128,2,1024]{2,1,0:T(2,128)(2,1)S(1)} copy-done((bf16[128,2,1024]{2,1,0:T(2,128)(2,1)S(1)}, bf16[128,2,1024]{2,1,0:T(2,128)(2,1)}, u32[]{:S(2)}) %copy-start) | copy-done | bytes 524312
  1.0 0.4 copy_bitcast_fusion
  1.4 65.0 %shard_map.28 = bf16[4,2,128,1024]{3,2,1,0:T(8,128)(2,1)S(1)} custom-call(bf16[8,256,128]{2,1,0:T(8,128)(2,1)S(1)} %bitcast.8, bf16[8,128,1536]{2,1,0:T(8,128)(2,1)} %constant.2.clone.g_hbm), custom_call_target="tpu_custom_call" | custom-call | tf_op jit(solution)/shard_map/pallas_call | solution.py:351
  66.4 1.3 %copy.7 = bf16[4,2,128,1024]{3,2,1,0:T(8,128)(2,1)} copy(bf16[4,2,128,1024]{3,2,1,0:T(8,128)(2,1)S(1)} %shard_map.28) | data formatting | bytes 4194304
Async XLA Ops:
  0.0 1.0 %copy-start = (bf16[128,2,1024]{2,1,0:T(2,128)(2,1)S(1)}, bf16[128,2,1024]{2,1,0:T(2,128)(2,1)}, u32[]{:S(2)}) copy-start(bf16[128,2,1024]{2,1,0:T(2,128)(2,1)} %param.2) | copy-start | bytes 1572868
